TPU v7x, 32 devices: a whole 2x2x4 slice. The times are simulated.
32 devices in a mesh: groups: 2 (over y), dp: 4 (over z), tensor: 2 (over x), sub: 2 (over core).
Axes of the slice: x: 2, y: 2, z: 4, core: 2. Of those that a mesh axis runs over, the one named last changes fastest.
Arguments:
- val_hidden: bfloat16 [1024, 7168], P(('groups', 'dp', 'sub'), 'tensor'), parts along dimension 0, may hold values from -6 to 6
- val_cotan: bfloat16 [1024, 4096], P(('groups', 'dp', 'sub')), parts along dimension 0, may hold values from -6 to 6
- val_count: int32 [16], P(('groups', 'dp', 'sub')), parts along dimension 0, may hold values from 16 to 64, as said below
- train_hidden: bfloat16 [2048, 7168], P(('groups', 'dp', 'sub'), 'tensor'), parts along dimension 0, may hold values from -6 to 6
- train_cotan: bfloat16 [2048, 4096], P(('groups', 'dp', 'sub')), parts along dimension 0, may hold values from -6 to 6
- seq_len: int32 [32], P('groups'), parts along dimension 0, may hold values from 1 to 64, as said below
- seq_device: int32 [32], P('groups'), parts along dimension 0, may hold values from 0 to 7, as said below
Outputs:
- weighted_grad: bfloat16 [14336, 4096], P(('groups', 'tensor'), ('dp', 'sub')), parts along dimension 0
- seq_weight: float32 [32], P('groups'), parts along dimension 0
There are 2 independent parts, one for each index of `groups`. A program takes and returns all parts, laid end to end along the dimension named above; each array names one. Nothing has to cross between parts.
Inputs may be any that keep to these rules, and one draw needn't show every extreme that they name: `val_count`: the first data device has 16 live slots and the last data device has all 64 slots live. `seq_len`: the sequences of one device fill at most 128 slots; some device holds 2 sequences of length 64. `seq_device`: every data device holds exactly 2 sequences.
All inputs are finite; a program needn't handle non-finite values.
Results may differ from a plain program's by a relative error of at most 0.0046.
The roundings to bfloat16 on the way count: a program that leaves them out, or rounds other values in their place, can miss the bound.
Values may be sent and summed in bfloat16 or wider, within the bound.
A program may use at most 64 MiB of HBM per device.

v0:
```python
import jax
import jax.numpy as jnp
from jax import lax
from jax.sharding import PartitionSpec as P

D = 4096
FF = 7168


def membership(seq_len, seq_device, row_count, capacity):
    seq_order = jnp.arange(seq_len.shape[0], dtype=jnp.int32)
    shared = seq_device[:, None] == seq_device[None, :]
    earlier = seq_order[None, :] < seq_order[:, None]
    offset = jnp.sum(jnp.where(shared & earlier, seq_len[None, :], 0), axis=1)
    row_ids = jnp.arange(row_count, dtype=jnp.int32)
    holder = row_ids // capacity
    within = row_ids % capacity
    inside = (
        (seq_device[None, :] == holder[:, None])
        & (within[:, None] >= offset[None, :])
        & (within[:, None] < (offset + seq_len)[None, :])
    )
    return inside.astype(jnp.float32)


def shards(val_hidden, val_cotan, val_count, train_hidden, train_cotan, seq_len, seq_device):
    contract_rows = (((0,), (0,)), ((), ()))
    val_slots = val_hidden.shape[0]
    val_live = jnp.arange(val_slots, dtype=jnp.int32) < val_count[0]
    val_kept = jnp.where(val_live[:, None], val_hidden, jnp.zeros_like(val_hidden))
    val_columns, train_columns = (
        lax.all_to_all(val_cotan, ("dp", "sub"), split_axis=1, concat_axis=0, tiled=True),
        lax.all_to_all(train_cotan, ("dp", "sub"), split_axis=1, concat_axis=0, tiled=True),
    )
    val_every, train_every = (
        lax.all_gather(val_kept, ("dp", "sub"), axis=0, tiled=True),
        lax.all_gather(train_hidden, ("dp", "sub"), axis=0, tiled=True),
    )
    val_block = lax.dot_general(
        val_every, val_columns, contract_rows, preferred_element_type=jnp.float32
    )
    val_grad = val_block.astype(jnp.bfloat16)
    projected = jnp.dot(train_every, val_grad, preferred_element_type=jnp.float32)
    token_part = jnp.sum(projected * train_columns, axis=1)
    member = membership(seq_len, seq_device, train_every.shape[0], train_hidden.shape[0])
    part_align = jnp.dot(token_part, member, precision=lax.Precision.HIGHEST)
    count_local = val_count[0].astype(jnp.float32)
    val_total = lax.psum(count_local, ("dp", "sub"))
    align = lax.psum(part_align, ("dp", "tensor", "sub"))
    lengths = seq_len.astype(jnp.float32)
    score = align / jnp.sqrt(val_total * lengths * float(FF) * float(D))
    seq_weight = jax.nn.sigmoid(score)
    mass = jnp.sum(seq_weight * lengths)
    row_weight = jnp.dot(member, seq_weight, precision=lax.Precision.HIGHEST)
    weighted_cotan = (row_weight[:, None] * train_columns).astype(jnp.bfloat16)
    weighted = lax.dot_general(
        train_every, weighted_cotan, contract_rows, preferred_element_type=jnp.float32
    )
    weighted_grad = (weighted / jnp.sqrt(mass)).astype(jnp.bfloat16)
    return (weighted_grad, seq_weight)


def solution(mesh):
    return jax.shard_map(
        shards,
        mesh=mesh,
        in_specs=(
            P(("groups", "dp", "sub"), "tensor"),
            P(("groups", "dp", "sub"), None),
            P(("groups", "dp", "sub")),
            P(("groups", "dp", "sub"), "tensor"),
            P(("groups", "dp", "sub"), None),
            P("groups"),
            P("groups"),
        ),
        out_specs=(P(("groups", "tensor"), ("dp", "sub")), P("groups")),
        check_vma=False,
    )
```

profile of v0, /device:TPU:0, one launch (start us, length us, event | category | flops | bytes accessed | tf_op | source)
XLA Modules:
  0.0 231.7 jit_solution(12047744341904695969)
XLA Ops:
  7.2 0.0 copy-start
  7.2 0.0 all-gather.3.cloned.1.call-start
  7.9 1.9 broadcast_select_fusion
  9.8 0.0 all-gather.3.cloned.1.call-update
  9.8 0.0 copy-start.1
  9.9 0.0 copy-start.2
  9.9 0.0 all-gather.5.cloned.1.call-start
  9.9 0.7 all-gather.5.cloned.1.call-update
  10.6 2.3 copy.22
  12.9 6.3 %all-to-all-start.1 = ((bf16[128,8,512]{0,2,1:T(8,128)(2,1)}), bf16[128,8,512]{0,2,1:T(8,128)(2,1)S(1)}, u32[]{:S(2)}, u32[]{:S(2)}) async-start(bf16[128,8,512]{0,2,1:T(8,128)(2,1)} %bitcast.4), calls=%async_computation.1 | async-start | bytes 2097152 | tf_op jit(solution)/shard_map/all_to_all | solution.py:33
  19.2 0.0 copy-done
  19.2 0.8 copy.28
  20.1 51.4 %all-to-all-done.1 = bf16[128,8,512]{0,2,1:T(8,128)(2,1)S(1)} async-done(((bf16[128,8,512]{0,2,1:T(8,128)(2,1)}), bf16[128,8,512]{0,2,1:T(8,128)(2,1)S(1)}, u32[]{:S(2)}, u32[]{:S(2)}) %all-to-all-start.1) | async-done | bytes 1048608 | tf_op jit(solution)/shard_map/all_to_all | solution.py:33
  71.5 3.5 %all-to-all-start = ((bf16[64,8,512]{2,0,1:T(8,128)(2,1)}), bf16[64,8,512]{2,0,1:T(8,128)(2,1)S(1)}, u32[]{:S(2)}, u32[]{:S(2)}) async-start(bf16[64,8,512]{2,0,1:T(8,128)(2,1)} %bitcast.29), calls=%async_computation | async-start | bytes 1048576 | tf_op jit(solution)/shard_map/all_to_all | solution.py:32
  75.0 0.0 copy-done.1
  75.0 0.0 copy-done.2
  75.0 0.2 select_reduce_fusion
  75.2 1.5 convert_bitcast_fusion
  76.7 1.9 copy.23
  78.6 1.8 copy.24
  80.4 13.4 %all-to-all-done = bf16[64,8,512]{2,0,1:T(8,128)(2,1)S(1)} async-done(((bf16[64,8,512]{2,0,1:T(8,128)(2,1)}), bf16[64,8,512]{2,0,1:T(8,128)(2,1)S(1)}, u32[]{:S(2)}, u32[]{:S(2)}) %all-to-all-start) | async-done | bytes 524320 | tf_op jit(solution)/shard_map/all_to_all | solution.py:32
  93.8 0.0 all-gather.3.cloned.1.call-done
  93.8 57.7 %all-gather.5.cloned.1.call-done = bf16[1024,3584]{1,0:T(8,128)(2,1)} async-done(((bf16[128,3584]{1,0:T(8,128)(2,1)}), bf16[1024,3584]{1,0:T(8,128)(2,1)}) %all-gather.5.cloned.1.call-update) | async-done | bytes 7340048 | tf_op jit(solution)/shard_map/all_gather | solution.py:37
  151.4 10.6 %fusion.1 = f32[1024]{0:T(1024)S(1)} fusion(f32[1024,512]{0,1:T(8,128)} %copy.24, bf16[1024,3584]{1,0:T(8,128)(2,1)} %all-gather.5.cloned.1.call-done, bf16[512,3584]{1,0:T(8,128)(2,1)} %all-gather.3.cloned.1.call-done, bf16[512,512]{1,0:T(8,128)(2,1)S(1)} %bitcast.35), kind=kOutput, calls=%fused_computation.4 | convolution fusion | flops 5640027136 | bytes 13635584 | tf_op jit(solution)/shard_map/dot_general | solution.py:43
  162.1 0.5 convolution_bitcast_fusion
  162.6 15.1 %psum.15 = f32[]{:T(128)} all-reduce(f32[]{:T(128)S(6)} %convert_element_type.33), channel_id=1, replica_groups=mesh['groups'=2,'dp'=4,'tensor'=2,'sub'=2] {'dp','sub'}, use_global_device_ids=true, to_apply=%region_3.4 | all-reduce | flops 1 | bytes 8 | tf_op jit(solution)/shard_map/psum | solution.py:48
  177.7 29.9 %psum.14 = f32[16]{0:T(128)S(1)} all-reduce(f32[16]{0:T(128)S(1)} %convolution_bitcast_fusion), channel_id=1, replica_groups=mesh['groups'=2,'dp'=4,'tensor'=2,'sub'=2] {'dp','tensor','sub'}, use_global_device_ids=true, to_apply=%region_2.3 | all-reduce | flops 16 | bytes 128 | tf_op jit(solution)/shard_map/psum | solution.py:49
  207.6 1.3 multiply_reduce_fusion
  208.9 0.0 copy-start.3
  209.6 0.6 fusion.3
  210.2 8.8 %fusion = bf16[3584,512]{0,1:T(8,128)(2,1)} fusion(bf16[1024,3584]{1,0:T(8,128)(2,1)} %all-gather.5.cloned.1.call-done, f32[]{:T(128)S(6)} %sqrt.7, f32[1024,512]{1,0:T(8,128)S(1)} %bitcast.33, f32[1024]{0:T(1024)S(1)} %bitcast.36), kind=kOutput, calls=%fused_computation.2 | convolution fusion | flops 3762814976 | bytes 13111300 | tf_op jit(solution)/shard_map/dot_general | solution.py:56
  219.0 0.0 copy-done.3
  219.0 5.9 %copy.25 = bf16[3584,512]{1,0:T(8,128)(2,1)} copy(bf16[3584,512]{0,1:T(8,128)(2,1)} %fusion) | data formatting | bytes 7340032
  (3 shorter events, 0.0 us)
Async XLA Ops:
  7.2 12.0 %copy-start = (bf16[64,4096]{1,0:T(8,128)(2,1)S(1)}, bf16[64,4096]{1,0:T(8,128)(2,1)}, u32[]{:S(2)}) copy-start(bf16[64,4096]{1,0:T(8,128)(2,1)} %param.8) | copy-start | bytes 1572868
  7.2 86.6 %all-gather.3.cloned.1.call-start = ((), (), s32[]{:S(2)}) async-start(), calls=%async_computation.2 | async-start | bytes 4128768 | tf_op jit(solution)/shard_map/all_gather | solution.py:36
  9.8 65.2 %copy-start.1 = (s32[16]{0:T(128)S(1)}, s32[16]{0:T(128)}, u32[]{:S(2)}) copy-start(s32[16]{0:T(128)} %param.12) | copy-start | bytes 196
  9.9 65.2 %copy-start.2 = (s32[16]{0:T(128)S(1)}, s32[16]{0:T(128)}, u32[]{:S(2)}) copy-start(s32[16]{0:T(128)} %param.13) | copy-start | bytes 196
  9.9 141.6 %all-gather.5.cloned.1.call-start = ((), (), s32[]{:S(2)}) async-start(), calls=%async_computation.3 | async-start | bytes 8257536 | tf_op jit(solution)/shard_map/all_gather | solution.py:37
  12.9 58.6 %all-to-all-start.1 = ((bf16[128,8,512]{0,2,1:T(8,128)(2,1)}), bf16[128,8,512]{0,2,1:T(8,128)(2,1)S(1)}, u32[]{:S(2)}, u32[]{:S(2)}) async-start(bf16[128,8,512]{0,2,1:T(8,128)(2,1)} %bitcast.4), calls=%async_computation.1 | async-start | bytes 2097152 | tf_op jit(solution)/shard_map/all_to_all | solution.py:33
  71.5 22.3 %all-to-all-start = ((bf16[64,8,512]{2,0,1:T(8,128)(2,1)}), bf16[64,8,512]{2,0,1:T(8,128)(2,1)S(1)}, u32[]{:S(2)}, u32[]{:S(2)}) async-start(bf16[64,8,512]{2,0,1:T(8,128)(2,1)} %bitcast.29), calls=%async_computation | async-start | bytes 1048576 | tf_op jit(solution)/shard_map/all_to_all | solution.py:32
  208.9 10.1 %copy-start.3 = (f32[16]{0:T(128)}, f32[16]{0:T(128)S(1)}, u32[]{:S(2)}) copy-start(f32[16]{0:T(128)S(1)} %get-tuple-element.13) | copy-start | bytes 196
Sparse Core Ops, SparseCore 0:
  10.0 66.9 all-gather.2
  78.6 72.7 all-gather.4
where the time goes:
time: 232 us
  waiting for transfers between devices  123 us (53%)
  blocking collectives  45 us (19%)
  matrix products  20.5 us (9%)
  between operations  15.5 us (7%)
  local copies, waits for them, and re-layouts  12.8 us (6%)
  starting transfers between devices  9.9 us (4%)
  other arithmetic  4.81 us (2%)
    all_gather x1, waiting for transfers between devices, shards(): lax.all_gather(train_hidden, ('dp', 'sub'), axis=0, tiled=True)  57.7 us
    all_to_all x1, waiting for transfers between devices, shards(): lax.all_to_all(train_cotan, ('dp', 'sub'), split_axis=1, concat_axis=0, t...  51.4 us
    psum x1, blocking collectives, shards(): align = lax.psum(part_align, ('dp', 'tensor', 'sub'))  29.9 us
    psum x1, blocking collectives, shards(): val_total = lax.psum(count_local, ('dp', 'sub'))  15.1 us
    all_to_all x1, waiting for transfers between devices, shards(): lax.all_to_all(val_cotan, ('dp', 'sub'), split_axis=1, concat_axis=0, til...  13.4 us
    dot_general x1, matrix products, shards(): jnp.dot(train_every, val_grad, preferred_element_type=jnp.float32)  10.6 us
    dot_general x1, matrix products, shards(): lax.dot_general(train_every, weighted_cotan, contract_rows, preferred_ele...  8.79 us
    unnamed x10, local copies, waits for them, and re-layouts  8.21 us
  transfers between devices with their start and end apart: 4, of which 3 were waited for; matrix products, arithmetic and copies ran while one was open for 4% of the time, Pallas kernels for 0%

commit v1 on v0

--- a/solution.py
+++ b/solution.py
@@ -46,7 +46,7 @@
     part_align = jnp.dot(token_part, member, precision=lax.Precision.HIGHEST)
     count_local = val_count[0].astype(jnp.float32)
     val_total = lax.psum(count_local, ("dp", "sub"))
-    align = lax.psum(part_align, ("dp", "tensor", "sub"))
+    align = lax.psum(lax.psum(part_align, ("tensor", "sub")), "dp")
     lengths = seq_len.astype(jnp.float32)
     score = align / jnp.sqrt(val_total * lengths * float(FF) * float(D))
     seq_weight = jax.nn.sigmoid(score)

time: 232 us -> 204 us (0.88)
  waiting for transfers between devices: 123 us -> 102 us
  blocking collectives: 45 us -> 38.3 us
    all_to_all x1, waiting for transfers between devices: 13.4 us -> 0.01 us  [shards(): lax.all_to_all(val_cotan, ('dp', 'sub'), split_axis=1, concat_axis=0, til...]
    psum x1 -> x2, blocking collectives: 29.9 us -> 16.6 us  [shards(): align = lax.psum(lax.psum(part_align, ('tensor', 'sub')), 'dp')]
    all_gather x1, waiting for transfers between devices: 57.7 us -> 49.5 us  [shards(): lax.all_gather(train_hidden, ('dp', 'sub'), axis=0, tiled=True)]
    psum x1, blocking collectives: 15.1 us -> 21.7 us  [shards(): val_total = lax.psum(count_local, ('dp', 'sub'))]
  transfers between devices with their start and end apart: 4 -> 4, of which waited for: 3 -> 2; matrix products, arithmetic and copies ran while one was open for 4% -> 4% of each run, Pallas kernels for 0% -> 0%
where the time goes in v1:
time: 204 us
  waiting for transfers between devices  102 us (50%)
  blocking collectives  38.3 us (19%)
  matrix products  20.5 us (10%)
  between operations  15.5 us (8%)
  local copies, waits for them, and re-layouts  12.9 us (6%)
  starting transfers between devices  9.9 us (5%)
  other arithmetic  4.82 us (2%)
    all_to_all x1, waiting for transfers between devices, shards(): lax.all_to_all(train_cotan, ('dp', 'sub'), split_axis=1, concat_axis=0, t...  51.4 us
    all_gather x1, waiting for transfers between devices, shards(): lax.all_gather(train_hidden, ('dp', 'sub'), axis=0, tiled=True)  49.5 us
    psum x1, blocking collectives, shards(): val_total = lax.psum(count_local, ('dp', 'sub'))  21.7 us
    psum x2, blocking collectives, shards(): align = lax.psum(lax.psum(part_align, ('tensor', 'sub')), 'dp')  16.6 us
    dot_general x1, matrix products, shards(): jnp.dot(train_every, val_grad, preferred_element_type=jnp.float32)  10.6 us
    dot_general x1, matrix products, shards(): lax.dot_general(train_every, weighted_cotan, contract_rows, preferred_ele...  8.78 us
    unnamed x10, local copies, waits for them, and re-layouts  8.21 us
    all_to_all x1, starting transfers between devices, shards(): lax.all_to_all(train_cotan, ('dp', 'sub'), split_axis=1, concat_axis=0, t...  6.33 us
  transfers between devices with their start and end apart: 4, of which 2 were waited for; matrix products, arithmetic and copies ran while one was open for 4% of the time, Pallas kernels for 0%

profile of v1, /device:TPU:0, one launch (start us, length us, event | category | flops | bytes accessed | tf_op | source)
XLA Modules:
  0.0 203.5 jit_solution(12670689197034346567)
XLA Ops:
  7.2 0.0 copy-start
  7.2 0.0 all-gather.3.cloned.1.call-start
  7.9 1.9 broadcast_select_fusion
  9.8 0.0 all-gather.3.cloned.1.call-update
  9.8 0.0 copy-start.1
  9.9 0.0 copy-start.2
  9.9 0.0 all-gather.5.cloned.1.call-start
  9.9 0.7 all-gather.5.cloned.1.call-update
  10.6 2.3 %copy.22 = bf16[128,4096]{0,1:T(8,128)(2,1)} copy(bf16[128,4096]{1,0:T(8,128)(2,1)} %param.11) | data formatting | bytes 2097152 | tf_op args[4]
  12.9 6.3 %all-to-all-start.1 = ((bf16[128,8,512]{0,2,1:T(8,128)(2,1)}), bf16[128,8,512]{0,2,1:T(8,128)(2,1)S(1)}, u32[]{:S(2)}, u32[]{:S(2)}) async-start(bf16[128,8,512]{0,2,1:T(8,128)(2,1)} %bitcast.4), calls=%async_computation.1 | async-start | bytes 2097152 | tf_op jit(solution)/shard_map/all_to_all | solution.py:33
  19.2 0.0 copy-done
  19.2 0.9 copy.28
  20.1 51.4 %all-to-all-done.1 = bf16[128,8,512]{0,2,1:T(8,128)(2,1)S(1)} async-done(((bf16[128,8,512]{0,2,1:T(8,128)(2,1)}), bf16[128,8,512]{0,2,1:T(8,128)(2,1)S(1)}, u32[]{:S(2)}, u32[]{:S(2)}) %all-to-all-start.1) | async-done | bytes 1048608 | tf_op jit(solution)/shard_map/all_to_all | solution.py:33
  71.5 3.5 %all-to-all-start = ((bf16[64,8,512]{2,0,1:T(8,128)(2,1)}), bf16[64,8,512]{2,0,1:T(8,128)(2,1)S(1)}, u32[]{:S(2)}, u32[]{:S(2)}) async-start(bf16[64,8,512]{2,0,1:T(8,128)(2,1)} %bitcast.29), calls=%async_computation | async-start | bytes 1048576 | tf_op jit(solution)/shard_map/all_to_all | solution.py:32
  75.0 21.7 %psum.23 = f32[]{:T(128)} all-reduce(f32[]{:T(128)S(6)} %convert_element_type.33), channel_id=1, replica_groups=mesh['groups'=2,'dp'=4,'tensor'=2,'sub'=2] {'dp','sub'}, use_global_device_ids=true, to_apply=%region_4.5 | all-reduce | flops 1 | bytes 8 | tf_op jit(solution)/shard_map/psum | solution.py:48
  96.7 0.0 copy-done.1
  96.7 0.0 copy-done.2
  96.7 0.2 select_reduce_fusion
  96.9 1.5 convert_bitcast_fusion
  98.4 2.0 copy.23
  100.4 1.8 copy.24
  102.2 0.0 all-to-all-done
  102.2 0.0 all-gather.3.cloned.1.call-done
  102.2 49.5 %all-gather.5.cloned.1.call-done = bf16[1024,3584]{1,0:T(8,128)(2,1)} async-done(((bf16[128,3584]{1,0:T(8,128)(2,1)}), bf16[1024,3584]{1,0:T(8,128)(2,1)}) %all-gather.5.cloned.1.call-update) | async-done | bytes 7340048 | tf_op jit(solution)/shard_map/all_gather | solution.py:37
  151.7 10.6 %fusion.1 = f32[1024]{0:T(1024)S(1)} fusion(f32[1024,512]{0,1:T(8,128)} %copy.24, bf16[1024,3584]{1,0:T(8,128)(2,1)} %all-gather.5.cloned.1.call-done, bf16[512,3584]{1,0:T(8,128)(2,1)} %all-gather.3.cloned.1.call-done, bf16[512,512]{1,0:T(8,128)(2,1)S(1)} %bitcast.35), kind=kOutput, calls=%fused_computation.4 | convolution fusion | flops 5640027136 | bytes 13635584 | tf_op jit(solution)/shard_map/dot_general | solution.py:43
  162.3 0.5 convolution_bitcast_fusion
  162.9 7.0 %psum.21 = f32[16]{0:T(128)S(1)} all-reduce(f32[16]{0:T(128)S(1)} %convolution_bitcast_fusion), channel_id=1, replica_groups=mesh['groups'=2,'dp'=4,'tensor'=2,'sub'=2] {'tensor','sub'}, use_global_device_ids=true, to_apply=%region_2.3 | all-reduce | flops 16 | bytes 128 | tf_op jit(solution)/shard_map/psum | solution.py:49
  169.9 9.6 %psum.22 = f32[16]{0:T(128)S(1)} all-reduce(f32[16]{0:T(128)S(1)} %psum.21), channel_id=1, replica_groups=mesh['groups'=2,'dp'=4,'tensor'=2,'sub'=2] {'dp'}, use_global_device_ids=true, to_apply=%region_3.4 | all-reduce | flops 16 | bytes 128 | tf_op jit(solution)/shard_map/psum | solution.py:49
  179.4 1.3 multiply_reduce_fusion
  180.7 0.0 copy-start.3
  181.4 0.6 fusion.3
  182.0 8.8 %fusion = bf16[3584,512]{0,1:T(8,128)(2,1)} fusion(bf16[1024,3584]{1,0:T(8,128)(2,1)} %all-gather.5.cloned.1.call-done, f32[]{:T(128)S(6)} %sqrt.7, f32[1024,512]{1,0:T(8,128)S(1)} %bitcast.33, f32[1024]{0:T(1024)S(1)} %bitcast.36), kind=kOutput, calls=%fused_computation.2 | convolution fusion | flops 3762814976 | bytes 13111300 | tf_op jit(solution)/shard_map/dot_general | solution.py:56
  190.7 0.0 copy-done.3
  190.7 5.9 %copy.25 = bf16[3584,512]{1,0:T(8,128)(2,1)} copy(bf16[3584,512]{0,1:T(8,128)(2,1)} %fusion) | data formatting | bytes 7340032
  (3 shorter events, 0.0 us)
Async XLA Ops:
  7.2 12.1 %copy-start = (bf16[64,4096]{1,0:T(8,128)(2,1)S(1)}, bf16[64,4096]{1,0:T(8,128)(2,1)}, u32[]{:S(2)}) copy-start(bf16[64,4096]{1,0:T(8,128)(2,1)} %param.8) | copy-start | bytes 1572868
  7.2 95.0 %all-gather.3.cloned.1.call-start = ((), (), s32[]{:S(2)}) async-start(), calls=%async_computation.2 | async-start | bytes 4128768 | tf_op jit(solution)/shard_map/all_gather | solution.py:36
  9.8 86.9 %copy-start.1 = (s32[16]{0:T(128)S(1)}, s32[16]{0:T(128)}, u32[]{:S(2)}) copy-start(s32[16]{0:T(128)} %param.12) | copy-start | bytes 196
  9.9 86.9 %copy-start.2 = (s32[16]{0:T(128)S(1)}, s32[16]{0:T(128)}, u32[]{:S(2)}) copy-start(s32[16]{0:T(128)} %param.13) | copy-start | bytes 196
  9.9 141.8 %all-gather.5.cloned.1.call-start = ((), (), s32[]{:S(2)}) async-start(), calls=%async_computation.3 | async-start | bytes 8257536 | tf_op jit(solution)/shard_map/all_gather | solution.py:37
  12.9 58.6 %all-to-all-start.1 = ((bf16[128,8,512]{0,2,1:T(8,128)(2,1)}), bf16[128,8,512]{0,2,1:T(8,128)(2,1)S(1)}, u32[]{:S(2)}, u32[]{:S(2)}) async-start(bf16[128,8,512]{0,2,1:T(8,128)(2,1)} %bitcast.4), calls=%async_computation.1 | async-start | bytes 2097152 | tf_op jit(solution)/shard_map/all_to_all | solution.py:33
  71.5 30.7 %all-to-all-start = ((bf16[64,8,512]{2,0,1:T(8,128)(2,1)}), bf16[64,8,512]{2,0,1:T(8,128)(2,1)S(1)}, u32[]{:S(2)}, u32[]{:S(2)}) async-start(bf16[64,8,512]{2,0,1:T(8,128)(2,1)} %bitcast.29), calls=%async_computation | async-start | bytes 1048576 | tf_op jit(solution)/shard_map/all_to_all | solution.py:32
  180.7 10.1 %copy-start.3 = (f32[16]{0:T(128)}, f32[16]{0:T(128)S(1)}, u32[]{:S(2)}) copy-start(f32[16]{0:T(128)S(1)} %get-tuple-element.13) | copy-start | bytes 196
Sparse Core Ops, SparseCore 0:
  10.0 66.9 all-gather.2
  78.6 73.0 all-gather.4
